TPU v7x, 32 devices: a whole 2x2x4 slice. The times are simulated.
32 devices in a mesh: image: 2 (over y), brick: 4 (over z), probe: 2 (over x), chan: 2 (over core).
Axes of the slice: x: 2, y: 2, z: 4, core: 2. Of those that a mesh axis runs over, the one named last changes fastest.
Arguments:
- atom_s: bfloat16 [2048, 128], P(('image', 'brick', 'probe'), 'chan'), parts along dimension 0, may hold values from -6 to 6
- atom_pos: float32 [3, 2048], P(None, ('image', 'brick', 'probe')), parts along dimension 1, may hold values from 0 to 4
- edge_vec: float32 [3, 32768], P(None, ('image', 'brick', 'probe')), parts along dimension 1, may hold values from -5 to 5, as said below
- edge_nbr: int32 [32768], P(('image', 'brick', 'probe')), parts along dimension 0, may hold values from 0 to 191
- border_index: int32 [1024], P(('image', 'brick', 'probe')), parts along dimension 0, may hold values from 0 to 127
- send_index: int32 [16, 32], P(('image', 'brick', 'probe')), parts along dimension 0, may hold values from 0 to 127
- probe_list: int32 [64, 128], P(('image', 'brick', 'probe')), parts along dimension 0, may hold values from 0 to 31
- probe_count: int32 [64], P(('image', 'brick', 'probe')), parts along dimension 0, may hold values from 64 to 128, as said below
- w_in: bfloat16 [2, 128, 128], replicated, may hold values from -0.5 to 0.5
- b_in: float32 [2, 128], replicated, may hold values from -3 to 3
- w_msg: bfloat16 [2, 128, 3, 128], P(None, None, None, 'chan'), may hold values from -0.5 to 0.5
- w_rad: bfloat16 [2, 16, 3, 128], P(None, None, None, 'chan'), may hold values from -1.5 to 1.5
- w_probe: bfloat16 [16, 2, 128], P(None, None, 'chan'), may hold values from -0.5 to 0.5
- w_mix: bfloat16 [128, 128], replicated, may hold values from -0.5 to 0.5
- b_mix: float32 [128], replicated, may hold values from -3 to 3
- w_out: float32 [128], replicated, may hold values from -0.5 to 0.5
Outputs:
- density: float32 [8192], P(('image', 'brick', 'probe')), parts along dimension 0
There are 2 independent parts, one for each index of `image`. A program takes and returns all parts, laid end to end along the dimension named above; an argument that names none is the same for every part. Nothing has to cross between parts.
Inputs may be any that keep to these rules, and one draw needn't show every extreme that they name: `edge_vec`: edge displacements have lengths between 1 and 5. `probe_count`: in every group some block has all 128 entries live.
All inputs are finite; a program needn't handle non-finite values.
Results may differ from a plain program's by a relative error of at most 0.012.
Values may be sent and summed in bfloat16 or wider, within the bound.
No kernel may reach another device: no remote copies, remote signals or barrier semaphores. Data moves between devices by JAX's collectives and lax.ppermute only.
A program may use at most 64 MiB of HBM per device.

v0:
```python
import functools
import itertools
import math

import jax
import jax.numpy as jnp
from jax import lax
from jax.experimental import pallas as pl
from jax.experimental.pallas import tpu as pltpu
from jax.sharding import PartitionSpec as P

PB = 128
LANES = 128
FEW_GROUPS = 8
SMALL = 16
TOGETHER = 2
ROOT = (2.0 * math.log2(math.e)) ** 0.5
F32 = jnp.float32
BF16 = jnp.bfloat16


def iota(shape, dim):
    return lax.broadcasted_iota(jnp.int32, shape, dim)


def dot(a, b):
    return jnp.dot(a, b, preferred_element_type=F32)


def dot_tn(a, b):
    return lax.dot_general(a, b, (((0,), (0,)), ((), ())), preferred_element_type=F32)


def one_hot(mask):
    return jnp.where(mask, 1.0, 0.0).astype(BF16)


def same(names, row):
    return jnp.where(names == row, jnp.ones_like(names), jnp.zeros_like(names))


def silu(x):
    half_x = 0.5 * x
    return half_x * jnp.tanh(half_x) + half_x


def bell(scaled, center):
    away = scaled - center
    return jnp.exp2(-(away * away))


def lane_atom(lane, fan, tiles):
    return (lane % tiles) * (LANES // fan) + lane // tiles


def length_keeping_round(exact):
    choices = []
    for value in exact:
        near = value.astype(BF16).astype(F32)
        step = jnp.where(value > near, 1.01 / 256.0, -1.01 / 256.0) * jnp.abs(near)
        choices.append((near, (near + step).astype(BF16).astype(F32)))
    target = sum(value * value for value in exact)
    best, best_error = None, None
    for picked in itertools.product(*choices):
        error = jnp.abs(sum(value * value for value in picked) - target)
        if best is None:
            best, best_error = picked, error
            continue
        better = error < best_error
        best = tuple(jnp.where(better, new, old) for new, old in zip(picked, best))
        best_error = jnp.where(better, error, best_error)
    return best


def pack_kernel(
    fan, atom_s, atom_pos, edge_vec, edge_nbr, border, send, w_msg, w_rad, w_probe,
    b_in, b_mix, w_out, probe_list, probe_count, data_out, weight_out, small_out, natural,
):
    half, atoms = atom_s.shape
    tiles = atoms * fan // LANES
    per_tile = LANES // fan
    part = lax.axis_index("chan")
    perm = one_hot(lane_atom(iota((atoms, LANES), 1), fan, tiles) == iota((atoms, LANES), 0))
    scalars = dot(atom_s[...], perm).astype(BF16)
    for tile in range(tiles):
        for comp in range(3):
            natural[comp * tiles + tile : comp * tiles + tile + 1, :] = edge_vec[
                comp : comp + 1, tile * LANES : (tile + 1) * LANES
            ]
    exact = [natural[comp * tiles : (comp + 1) * tiles, :] for comp in range(3)]
    for comp, value in enumerate(length_keeping_round(exact)):
        natural[comp * tiles : (comp + 1) * tiles, :] = value
    natural[3 * tiles : 4 * tiles, :] = edge_nbr[...].astype(F32)
    natural[4 * tiles :, :] = jnp.zeros((LANES - 4 * tiles, LANES), F32)
    turned = natural[...].T
    lane = iota((fan, LANES), 1)
    sorted_rows = []
    for comp in range(4):
        rows = jnp.zeros((fan, LANES), F32)
        for a in range(per_tile):
            piece = turned[a * fan : (a + 1) * fan, :]
            shift = (a * tiles - comp * tiles) % LANES
            piece = pltpu.roll(piece, shift, 1) if shift else piece
            rows = jnp.where(lane // tiles == a, piece, rows)
        sorted_rows.append(rows)
    blank = jnp.zeros((1, LANES), F32)
    every_edge = jnp.concatenate(sorted_rows, axis=0).astype(BF16)
    sorted_rows = [jnp.where(part == 0, rows[: fan // 2], rows[fan // 2 :]) for rows in sorted_rows]
    border_row = jnp.concatenate(
        [border[...].astype(F32), jnp.zeros((1, LANES - border.shape[1]), F32)], axis=1
    )
    picks = send.shape[1]
    groups = data_out.shape[0]
    cap = picks // groups
    block = fan * cap
    lane = iota((picks, groups * block), 1)
    place = (lane // block) * cap + lane % cap
    send_row = jnp.broadcast_to(send[...].astype(F32), (8, picks)).astype(BF16)
    wanted = dot(send_row, one_hot(iota((picks, groups * block), 0) == place))[0:1]
    atom_col = lane_atom(iota((LANES, groups * block), 0), fan, tiles).astype(F32)
    spread = dot(every_edge, one_hot(atom_col == wanted))
    edge_k = iota(spread.shape, 0) % fan
    spread = jnp.where(edge_k == (iota(spread.shape, 1) % block) // cap, spread, 0.0)
    picked = jnp.sum(spread.reshape(4, fan, groups * block), axis=1)
    pick_atom = one_hot(iota((atoms, picks), 0).astype(F32) == send[...].astype(F32))
    facts = [send[...].astype(F32)]
    pos = dot(atom_pos[...].astype(BF16), pick_atom)
    facts += [pos[x : x + 1] for x in range(3)]
    owner = iota((groups, picks), 1) // cap == iota((groups, picks), 0)
    facts = jnp.concatenate([jnp.where(owner, fact, 0.0) for fact in facts], axis=1)
    row = iota((4 * picks, LANES), 0)
    place = (row // picks) * cap + row % cap
    facts = dot(facts.astype(BF16), one_hot(place == iota((4 * picks, LANES), 1)))
    edge_part = jnp.concatenate(sorted_rows, axis=0).astype(BF16)
    for group in range(groups):
        mine = slice(group * block, (group + 1) * block)
        rest = [facts[group : group + 1], border_row]
        for comp in (0, 2):
            rest.append(
                jnp.concatenate([picked[comp : comp + 1, mine], picked[comp + 1 : comp + 2, mine]], axis=1)
            )
        rest = jnp.concatenate(rest + [blank] * 4, axis=0)
        data_out[group, 0:half, :] = scalars
        data_out[group, half : half + 2 * fan, :] = edge_part
        data_out[group, half + 2 * fan :, :] = rest.astype(BF16)
    at = 0
    for piece in (b_in, b_mix, w_out, probe_list, probe_count):
        rows, cols = piece.shape
        small_out[at : at + rows, 0:cols] = piece[...].astype(F32)
        at += rows
    probe_rows = [w_probe[r].astype(F32) for r in range(w_probe.shape[0])]
    radial = jnp.concatenate([w_rad[...].astype(F32)] + probe_rows, axis=0).T.astype(BF16)
    weight_out[: w_msg.shape[0], :] = w_msg[...]
    weight_out[w_msg.shape[0] :, :] = radial


def pack(
    groups, atom_s, atom_pos, edge_vec, edge_nbr, border_index, send_index, w_msg, w_rad, w_probe,
    b_in, b_mix, w_out, probe_list, probe_count,
):
    atoms, half = atom_s.shape
    fan = edge_nbr.shape[0] // atoms
    return pl.pallas_call(
        functools.partial(pack_kernel, fan),
        out_shape=(
            jax.ShapeDtypeStruct((groups, half + 4 * fan // 2 + 8, LANES), BF16),
            jax.ShapeDtypeStruct((w_msg.size // LANES + half, LANES), BF16),
            jax.ShapeDtypeStruct((SMALL, LANES), F32),
        ),
        scratch_shapes=[pltpu.VMEM((LANES, LANES), F32)],
        name="pack",
    )(
        atom_s.T,
        atom_pos,
        edge_vec,
        edge_nbr.reshape(-1, LANES),
        border_index.reshape(1, -1),
        send_index,
        jnp.transpose(w_msg, (0, 2, 3, 1)).reshape(-1, LANES),
        jnp.transpose(w_rad, (0, 2, 1, 3)).reshape(-1, half),
        w_probe,
        b_in,
        b_mix.reshape(1, -1),
        w_out.reshape(1, -1),
        probe_list,
        probe_count.reshape(1, -1),
    )


def probe_grid(me, probes):
    number = me * probes + iota((1, probes), 1)
    return [(n % 16).astype(F32) * 0.25 - 1.875 for n in (number, number // 16, number // 256)]


def index_kernel(sizes, list_at, data_mine, small, facts_out, slots, probe_basis):
    groups, fan, rim, half, n_basis, cap, n_blocks = sizes
    tiles = fan
    received = groups * cap
    per_group = fan * cap
    edges = received * fan
    rest_at = half + 2 * fan
    me = lax.axis_index("brick") * lax.axis_size("probe") + lax.axis_index("probe")
    small_rows = small[...]
    rest = [data_mine[g, rest_at : rest_at + 8, :].astype(F32) for g in range(groups)]
    facts = jnp.concatenate([rows[0:1] for rows in rest], axis=0).astype(BF16)
    lane = iota((LANES, 4 * received), 1)
    wanted = (lane // received) * cap + lane % cap
    facts = dot(facts, one_hot(iota((LANES, 4 * received), 0) == wanted))
    source = (iota(facts.shape, 1) % received) // cap
    facts = jnp.sum(jnp.where(source == iota(facts.shape, 0), facts, 0.0), axis=0, keepdims=True)
    pick_atoms = facts[:, 0:received]
    for comp in range(3):
        rows = [r[2 + comp // 2 : 3 + comp // 2, (comp % 2) * per_group :][:, :per_group] for r in rest]
        facts_out[comp : comp + 1, :] = jnp.concatenate(rows, axis=1)
    nbr = jnp.concatenate([r[3:4, per_group : 2 * per_group] for r in rest], axis=1).astype(jnp.int32)

    home = iota((1, edges), 1) // per_group
    is_low = (nbr >= LANES) & (nbr < LANES + rim)
    is_up = nbr >= LANES + rim
    owner = jnp.where(
        is_low, (home + groups - 1) % groups, jnp.where(is_up, (home + 1) % groups, home)
    )
    entry = owner * 2 * rim + jnp.where(is_low, nbr - (LANES - rim), nbr - (LANES + rim))
    entry = jnp.where(is_low | is_up, entry, -1)
    border_all = jnp.concatenate([r[1:2, 0 : 2 * rim] for r in rest], axis=1)
    border_all = jnp.broadcast_to(border_all, (16, groups * 2 * rim)).astype(BF16)
    seen = dot(border_all, one_hot(iota((groups * 2 * rim, edges), 0) == entry))[0:1]
    target = jnp.where(entry < 0, nbr, seen.astype(jnp.int32))

    column = iota((groups * LANES, 1), 0)
    column_name = (column // LANES) * LANES + lane_atom(column % LANES, fan, tiles)
    home = iota((1, received), 1) // cap
    self_hot = one_hot(column_name == home * LANES + pick_atoms.astype(jnp.int32))
    uses = dot(self_hot, jnp.ones((received, LANES), BF16))
    uses = [uses[g * LANES : (g + 1) * LANES] for g in range(groups)]
    quad = groups // 2
    window_hot, near_groups = [], []
    for h in range(2):
        lanes = slice(h * edges // 2, (h + 1) * edges // 2)
        near = lax.rem(owner[:, lanes] + 2 * groups - (h * quad + groups - 1), groups)
        hot = one_hot(column_name[: (quad + 2) * LANES] == near * LANES + target[:, lanes])
        window_hot.append(hot)
        near_groups.append(near)
        used = dot(hot, jnp.ones((edges // 2, LANES), BF16))
        for i in range(quad + 2):
            g = (h * quad + groups - 1 + i) % groups
            uses[g] = uses[g] + used[i * LANES : (i + 1) * LANES]
    lane = iota((LANES, LANES), 1)
    needed = jnp.zeros((LANES, LANES), F32)
    for g in range(groups):
        needed = jnp.where((lane == g) & (uses[g] > 0.0), 1.0, needed)
    order = dot(one_hot(lane <= iota((LANES, LANES), 0)), needed.astype(BF16))
    slot = jnp.where(needed > 0.0, order - 1.0, -1.0)
    slots[...] = slot
    slot_rows = slot.T
    facts_out[8:9, 0:LANES] = order[LANES - 1 : LANES, :]

    for h in range(2):
        lanes = slice(h * edges // 2, (h + 1) * edges // 2)
        in_window = [(h * quad + groups - 1 + i) % groups for i in range(quad + 2)]
        row = jnp.concatenate([slot_rows[g : g + 1] for g in in_window], axis=1)
        row = jnp.broadcast_to(row, (16, (quad + 2) * LANES)).astype(BF16)
        place = dot(row, window_hot[h])[0:1]
        facts_out[3:4, lanes] = near_groups[h].astype(F32) * LANES + place
    row = jnp.concatenate([slot_rows[g : g + 1] for g in range(groups)], axis=1)
    row = jnp.broadcast_to(row, (16, groups * LANES)).astype(BF16)
    facts_out[7:8, 0:received] = home.astype(F32) * LANES + dot(row, self_hot)[0:1]

    shifted = facts - 1.875
    for x in range(3):
        facts_out[4 + x : 5 + x, 0:received] = shifted[:, (1 + x) * received : (2 + x) * received]
    pos_cols = jnp.broadcast_to(shifted, (LANES, 4 * received)).T
    list_len = LANES
    counts = []
    for block in range(n_blocks):
        limit = small_rows[list_at + n_blocks : list_at + n_blocks + 1, block : block + 1]
        live = iota((1, list_len), 1).astype(F32) < limit
        named = jnp.where(live, small_rows[list_at + block : list_at + block + 1], -1.0)
        hits = jnp.where(iota((received, list_len), 0).astype(F32) == named, 1.0, 0.0)
        counts.append(jnp.broadcast_to(jnp.sum(hits, axis=1, keepdims=True), (received, PB)))
    counts = jnp.concatenate(counts, axis=1)
    probes = n_blocks * PB
    grid = probe_grid(me, probes)
    dist_sq = jnp.zeros((received, probes), F32)
    for x in range(3):
        dist_sq = dist_sq + (grid[x] - pos_cols[(1 + x) * received : (2 + x) * received, 0:1]) ** 2
    dist = jnp.sqrt(dist_sq) * ROOT
    envelope = (1.0 - dist_sq / 64.0) ** 2 * counts
    probe_basis[...] = jnp.concatenate(
        [
            (bell(dist, r * (ROOT * 7.0 / (n_basis - 1))) * envelope).astype(BF16)
            for r in range(n_basis)
        ],
        axis=0,
    )


def density_kernel(
    sizes,
    data_mine,
    data_other,
    weights_mine,
    weights_other,
    small,
    w_in,
    w_mix,
    facts,
    slots,
    probe_basis,
    density,
    state0,
    own0,
    faces0,
    state1,
    weights,
):
    groups, fan, rim, half, n_basis, cap, n_blocks = sizes
    layers = w_in.shape[0]
    width = 2 * half
    tiles = LANES * fan // LANES
    root_fan = fan**0.5
    me = lax.axis_index("brick") * lax.axis_size("probe") + lax.axis_index("probe")
    part = lax.axis_index("chan")
    weights[part] = weights_mine[...]
    weights[1 - part] = weights_other[...]
    every = groups * LANES
    edge_at = half
    n_edge = 4 * fan // 2
    rest_at = half + n_edge

    def data(group, c, rows):
        return (data_mine, data_other)[c][group, rows, :]

    def weight(layer, p):
        at = (layer * 3 + p) * half
        return jnp.concatenate([weights[c, at : at + half, :] for c in range(2)], axis=0)

    def radial_weight(layer, p):
        at = (layer * 3 + p) * n_basis
        return radial_all[:, at : at + n_basis]

    def edge_rows(group):
        return [data(group, c, slice(edge_at, rest_at)).astype(F32) for c in range(2)]

    def border_of(group):
        return data(group, 0, slice(rest_at, rest_at + 8)).astype(F32)[1:2, 0 : 2 * rim]

    centers = iota((n_basis, 1), 0).astype(F32) * (ROOT * 6.0 / (n_basis - 1))

    def basis_of(length, env):
        return (bell(length * ROOT, centers) * env).astype(BF16)

    small_rows = small[...]
    columns = small_rows.T
    radial_at = weights.shape[1] - half
    radial_all = jnp.concatenate([weights[c, radial_at:, :] for c in range(2)], axis=0)

    received = groups * cap
    edges = received * fan
    per_group = fan * cap
    pick_vec = [facts[x : x + 1, :] for x in range(3)]
    pos = facts[4:7, 0:received]
    length = jnp.sqrt(sum(x * x for x in pick_vec))
    basis1 = basis_of(length, (1.0 - length * length / 36.0) ** 2)
    quad = groups // 2
    window = [[(h * quad + groups - 1 + i) % groups for i in range(quad + 2)] for h in range(2)]
    near_row = iota(((quad + 2) * LANES, edges // 2), 0).astype(F32)
    window_pick = [
        one_hot(near_row == facts[3:4, h * edges // 2 : (h + 1) * edges // 2]) for h in range(2)
    ]
    chosen_atoms = one_hot(iota((every, received), 0).astype(F32) == facts[7:8, 0:received])

    terms_shape = (2 * n_basis, n_basis * received)
    probe_weight = radial_all[:, 3 * layers * n_basis :]
    w_scalar, w_vector = (
        dot(probe_weight, one_hot(iota(terms_shape, 1) // received * 2 + p == iota(terms_shape, 0)))
        for p in range(2)
    )

    probes = density.shape[1]
    grid = probe_grid(me, probes)

    for group in range(groups):
        for c in range(2):
            place = part if c == 0 else 1 - part
            rows = pl.ds(pl.multiple_of(place * half, half), half)
            state0[rows, group * LANES : (group + 1) * LANES] = data(group, c, slice(0, half))
    hidden = silu(dot_tn(w_in[0], state0[...]) + columns[:, 0:1]).astype(BF16)
    weight_ac = jnp.concatenate([weight(0, 0), weight(0, 2)], axis=0)
    messages = dot(weight_ac, hidden).astype(BF16)
    atom_col = lane_atom(iota((LANES, 2 * rim), 0), fan, tiles).astype(F32)
    for group in range(groups):
        own = messages[:, group * LANES : (group + 1) * LANES]
        own0[group] = own
        border_row = border_of(group)
        faces0[group, :, 0 : 2 * rim] = dot(own, one_hot(atom_col == border_row)).astype(BF16)

    row = iota((LANES + 2 * rim, 1), 0)
    names = jnp.where(
        row < LANES,
        lane_atom(row, fan, tiles),
        jnp.where(row < LANES + rim, row + rim, row - rim),
    ).astype(F32)
    names = jnp.broadcast_to(names, (LANES + 2 * rim, LANES)).astype(BF16)
    upper_lane = iota((2 * width, 2 * rim), 1) < rim
    radial_ac = jnp.concatenate([radial_weight(0, 0), radial_weight(0, 2)], axis=0)
    radial_rows = jnp.concatenate([jnp.zeros((2 * width, LANES + 2 * rim), BF16), radial_ac], axis=1)
    blank = jnp.zeros((2 * width, n_basis), BF16)

    some = LANES // 2
    step = fan // 2

    def update(group, first_slot):
        up = (group + 1) % groups
        low = (group + groups - 1) % groups
        ghosts = jnp.where(
            upper_lane,
            faces0[up, :, 0 : 2 * rim].astype(F32),
            faces0[low, :, 0 : 2 * rim].astype(F32),
        ).astype(BF16)
        table = jnp.concatenate([own0[group], ghosts, blank], axis=1)
        left = jnp.concatenate(
            [
                block[at : at + 16]
                for at in range(0, 2 * width, 16)
                for block in (table, radial_rows)
            ],
            axis=0,
        )
        lanes = slice(group * LANES, (group + 1) * LANES)
        slot_lane = (iota((LANES, some), 1) + first_slot).astype(F32)
        in_slot = one_hot(slots[:, group : group + 1] == slot_lane)
        source = jnp.concatenate(
            [data(group, c, slice(edge_at, rest_at)) for c in range(2)] + [state0[:, lanes]], axis=0
        )
        source = dot(source, in_slot)
        rows = jnp.concatenate([source[:n_edge], source[n_edge : 2 * n_edge]], axis=1)
        own_scalars = source[2 * n_edge :]
        vec = [rows[x * step : (x + 1) * step] for x in range(3)]
        nbr = rows[3 * step : 4 * step]
        length = jnp.sqrt(vec[0] * vec[0] + vec[1] * vec[1] + vec[2] * vec[2])
        env = (1.0 - length * length / 36.0) ** 2
        acc = jnp.zeros((width, LANES), F32)
        acc_vec = [jnp.zeros((width, LANES), F32) for _ in range(3)]
        for first in range(0, step, TOGETHER):
            ks = range(first, first + TOGETHER)
            picked = jnp.concatenate([same(names, nbr[k : k + 1].astype(BF16)) for k in ks], axis=1)
            basis = jnp.concatenate(
                [basis_of(length[k : k + 1], env[k : k + 1]) for k in ks], axis=1
            )
            both = dot(left, jnp.concatenate([picked, basis], axis=0))
            prod = jnp.concatenate(
                [both[at : at + 16] * both[at + 16 : at + 32] for at in range(0, 4 * width, 32)],
                axis=0,
            )
            for i, k in enumerate(ks):
                block = prod[:, i * LANES : (i + 1) * LANES]
                acc = acc + block[:width]
                for x in range(3):
                    acc_vec[x] = acc_vec[x] + block[width:] * vec[x][k : k + 1]
        acc, *acc_vec = [(a[:, :some] + a[:, some:]) / root_fan for a in [acc] + acc_vec]
        return jnp.concatenate([own_scalars + acc] + acc_vec, axis=0)

    for group in range(groups):
        state = update(group, 0)
        state = jnp.concatenate([state, jnp.zeros_like(state)], axis=1)
        state1[:, group * LANES : (group + 1) * LANES] = state.astype(BF16)

    @pl.when(jnp.max(facts[8:9, 0:groups]) > some)
    def _():
        for group in range(groups):

            @pl.when(jnp.max(facts[8:9, group : group + 1]) > some)
            def _():
                lanes = slice(group * LANES + some, (group + 1) * LANES)
                state1[:, lanes] = update(group, some).astype(BF16)

    rows = []
    for h in range(2):
        near_states = jnp.concatenate(
            [state1[:, g * LANES : (g + 1) * LANES] for g in window[h]], axis=1
        )
        rows.append(dot(near_states, window_pick[h]))
    rows = jnp.concatenate(rows, axis=1)
    hidden = silu(dot_tn(w_in[1], rows[:width].astype(BF16)) + columns[:, 1:2]).astype(BF16)
    weight_abc = jnp.concatenate([weight(1, p) for p in range(3)], axis=0)
    messages = dot(weight_abc, hidden).astype(BF16).astype(F32)
    radial_abc = jnp.concatenate([radial_weight(1, p) for p in range(3)], axis=0)
    filters = dot(radial_abc, basis1)
    weighted = messages * filters
    gate = weighted[width : 2 * width]
    along = weighted[2 * width :]
    parts = [weighted[:width]]
    for x in range(3):
        parts.append(rows[(1 + x) * width : (2 + x) * width] * gate + along * pick_vec[x])
    parts = jnp.concatenate(parts, axis=0).astype(BF16)
    edge = iota((edges, received), 0)
    slot = (edge // per_group) * cap + edge % cap
    delta = dot(parts, one_hot(slot == iota((edges, received), 1)))
    final = (dot(state1[...], chosen_atoms) + delta / root_fan).astype(BF16).astype(F32)

    along = final[width : 2 * width] * pos[0:1]
    for x in range(1, 3):
        along = along + final[(x + 1) * width : (x + 2) * width] * pos[x : x + 1]
    def repeat(value):
        return jnp.concatenate([value] * n_basis, axis=1)
    terms = [w_scalar * repeat(final[:width]) - w_vector * repeat(along)]
    for x in range(3):
        terms.append(w_vector * repeat(final[(x + 1) * width : (x + 2) * width]))
    sums = dot(jnp.concatenate(terms, axis=0).astype(BF16), probe_basis[...])
    charges = sums[:width]
    for x in range(3):
        charges = charges + grid[x] * sums[(x + 1) * width : (x + 2) * width]
    mixed = dot_tn(w_mix[...], charges.astype(BF16)) + columns[:, layers : layers + 1]
    density[...] = jnp.sum(silu(mixed) * columns[:, layers + 1 : layers + 2], axis=0, keepdims=True)


def few_groups(
    atom_s, atom_pos, edge_vec, edge_nbr, border_index, send_index, probe_list, probe_count,
    w_in, b_in, w_msg, w_rad, w_probe, w_mix, b_mix, w_out,
):
    atoms, half = atom_s.shape
    groups = lax.axis_size("brick") * lax.axis_size("probe")
    fan = edge_nbr.shape[0] // atoms
    rim = border_index.shape[0] // 2
    n_basis = w_rad.shape[1]
    cap = send_index.shape[1] // groups
    width = 2 * half
    every = groups * LANES
    data, weights, small = pack(
        groups, atom_s, atom_pos, edge_vec, edge_nbr, border_index, send_index, w_msg, w_rad, w_probe,
        b_in, b_mix, w_out, probe_list, probe_count,
    )
    swap = [(0, 1), (1, 0)]
    weights_other = lax.ppermute(weights, "chan", swap)
    mine = lax.all_to_all(data, ("brick", "probe"), split_axis=0, concat_axis=0, tiled=True)
    other = lax.ppermute(mine, "chan", swap)
    n_probes = probe_list.shape[0] * PB
    sizes = (groups, fan, rim, half, n_basis, cap, probe_list.shape[0])
    facts, slots, probe_basis = pl.pallas_call(
        functools.partial(index_kernel, sizes, w_in.shape[0] + 2),
        out_shape=(
            jax.ShapeDtypeStruct((16, groups * cap * fan), F32),
            jax.ShapeDtypeStruct((LANES, LANES), F32),
            jax.ShapeDtypeStruct((n_basis * groups * cap, n_probes), BF16),
        ),
        compiler_params=pltpu.CompilerParams(vmem_limit_bytes=24 * 1024 * 1024),
        name="index",
    )(mine, small)
    density = pl.pallas_call(
        functools.partial(density_kernel, sizes),
        out_shape=jax.ShapeDtypeStruct((1, n_probes), F32),
        scratch_shapes=[
            pltpu.VMEM((width, every), BF16),
            pltpu.VMEM((groups, 2 * width, LANES), BF16),
            pltpu.VMEM((groups, 2 * width, LANES), BF16),
            pltpu.VMEM((4 * width, every), BF16),
            pltpu.VMEM((2,) + weights.shape, BF16),
        ],
        compiler_params=pltpu.CompilerParams(vmem_limit_bytes=40 * 1024 * 1024),
        name="density",
    )(mine, other, weights, weights_other, small, w_in, w_mix, facts, slots, probe_basis)
    return density.reshape(n_probes)


def per_device(*args):
    if lax.axis_size("brick") * lax.axis_size("probe") == FEW_GROUPS:
        return few_groups(*args)
    return many_groups(*args)


def extended(block, sides, width):
    for axis, dim in sides:
        count = lax.axis_size(axis)
        forward = [(i, i + 1) for i in range(count - 1)]
        forward.append((count - 1, 0))
        backward = [(target, source) for source, target in forward]
        low = lax.ppermute(
            lax.slice_in_dim(block, block.shape[dim] - width, None, axis=dim), axis, forward
        )
        high = lax.ppermute(lax.slice_in_dim(block, 0, width, axis=dim), axis, backward)
        block = jnp.concatenate([low, block, high], axis=dim)
    return block


def radial(distance, count, top):
    centers = jnp.arange(count).astype(jnp.float32) * (top / (count - 1))
    return jnp.exp(-2.0 * (distance[..., None] - centers) ** 2)


def make_block(
    recv_rows, recv_pos, w_scalar, w_vector, feat_width, group_no, n_blocks, list_len, n_basis
):

    def probe_block(block_in):
        block_no, listed, live_count = block_in
        index_row = (group_no * n_blocks + block_no) * PB + jnp.arange(PB, dtype=jnp.int32)
        grid_xyz = (
            jnp.stack([index_row % 16, index_row // 16 % 16, index_row // 256 % 16], axis=1).astype(
                jnp.float32
            )
            * 0.25
        )
        atom_xyz = recv_pos[:, listed]
        disp = grid_xyz[:, :, None] - atom_xyz[None]
        dist_sq = jnp.sum(disp * disp, axis=1)
        live = (jnp.arange(list_len, dtype=jnp.int32) < live_count).astype(jnp.float32)
        envelope = (1.0 - dist_sq / 64.0) ** 2 * live[None, :]
        basis = radial(jnp.sqrt(dist_sq), n_basis, 7.0) * envelope[:, :, None]
        scalar_w = basis.astype(jnp.bfloat16).reshape(PB, list_len * n_basis)
        vector_w = (
            (disp[:, :, :, None] * basis[:, None])
            .astype(jnp.bfloat16)
            .reshape(PB, 3 * list_len * n_basis)
        )
        atom_rows = recv_rows[listed]
        atom_terms = (atom_rows[:, None, :feat_width] * w_scalar[None]).reshape(
            list_len * n_basis, feat_width
        )
        vec_rows = jnp.transpose(
            atom_rows[:, feat_width:].reshape(list_len, 3, feat_width), (1, 0, 2)
        )
        vector_terms = (vec_rows[:, :, None, :] * w_vector[None, None]).reshape(
            3 * list_len * n_basis, feat_width
        )
        charge = jnp.dot(scalar_w, atom_terms, preferred_element_type=jnp.float32) + jnp.dot(
            vector_w, vector_terms, preferred_element_type=jnp.float32
        )
        return charge.astype(jnp.bfloat16)

    return probe_block


def many_groups(
    atom_s,
    atom_pos,
    edge_vec,
    edge_nbr,
    border_index,
    send_index,
    probe_list,
    probe_count,
    w_in,
    b_in,
    w_msg,
    w_rad,
    w_probe,
    w_mix,
    b_mix,
    w_out,
):
    atom_count, half_width = atom_s.shape
    n_layers = w_in.shape[0]
    width = w_in.shape[1]
    n_basis = w_rad.shape[1]
    fan_out = edge_nbr.shape[0] // atom_count
    root_fan = fan_out**0.5
    rim_rows = border_index.shape[0] // 2
    length = jnp.sqrt(jnp.sum(edge_vec * edge_vec, axis=0))
    edge_env = (1.0 - length * length / 36.0) ** 2
    edge_basis = (radial(length, n_basis, 6.0) * edge_env[:, None]).astype(jnp.bfloat16)
    edge_cols = jnp.transpose(edge_vec)
    scalars = atom_s
    vectors = jnp.zeros((atom_count, 3 * half_width), jnp.bfloat16)
    for layer_no in range(n_layers):
        full_rows = lax.all_gather(scalars, "chan", axis=1, tiled=True)
        in_weight = w_in[layer_no]
        in_bias = b_in[layer_no]
        msg_weight = w_msg[layer_no].reshape(width, 3 * half_width)
        rad_weight = w_rad[layer_no].reshape(n_basis, 3 * half_width)
        hidden_act = jax.nn.silu(
            jnp.dot(full_rows, in_weight, preferred_element_type=jnp.float32) + in_bias
        ).astype(jnp.bfloat16)
        inner_tab = jnp.concatenate(
            [
                jnp.dot(hidden_act, msg_weight, preferred_element_type=jnp.float32).astype(
                    jnp.bfloat16
                ),
                vectors,
            ],
            axis=1,
        )
        padded = extended(inner_tab[border_index], ((("brick", "probe"), 0),), rim_rows)
        lookup = jnp.concatenate([inner_tab, padded[:rim_rows], padded[3 * rim_rows :]], axis=0)
        neighbour_rows = lookup[edge_nbr]
        filters = jnp.dot(edge_basis, rad_weight, preferred_element_type=jnp.float32)
        weighted = neighbour_rows[:, : 3 * half_width] * filters
        neighbour_vec = neighbour_rows[:, 3 * half_width :].reshape(-1, 3, half_width)
        vector_gate = weighted[:, None, half_width : 2 * half_width]
        along_edge = weighted[:, None, 2 * half_width :]
        delta_vec = neighbour_vec * vector_gate + along_edge * edge_cols[:, :, None]
        delta_scalar = (
            weighted[:, :half_width].reshape(atom_count, fan_out, half_width).sum(axis=1) / root_fan
        )
        delta_vec = delta_vec.reshape(atom_count, fan_out, 3 * half_width).sum(axis=1) / root_fan
        scalars = (scalars + delta_scalar).astype(jnp.bfloat16)
        vectors = (vectors + delta_vec).astype(jnp.bfloat16)
    features = jnp.concatenate([scalars, vectors], axis=1)
    picks = send_index[0]
    n_brick = lax.axis_size("brick")
    n_probe = lax.axis_size("probe")
    n_groups = n_brick * n_probe
    slot_cap = picks.shape[0] // n_groups
    out_rows = features[picks]
    out_pos = jnp.transpose(atom_pos)[picks].astype(jnp.bfloat16)
    received = (
        lax.all_to_all(
            out_rows.reshape(n_groups, slot_cap, 4 * half_width),
            ("brick", "probe"),
            split_axis=0,
            concat_axis=0,
            tiled=True,
        ),
        lax.all_to_all(
            out_pos.reshape(n_groups, slot_cap, 3),
            ("brick", "probe"),
            split_axis=0,
            concat_axis=0,
            tiled=True,
        ),
    )
    recv_count = n_groups * slot_cap
    recv_rows = received[0].reshape(recv_count, 4 * half_width)
    recv_pos = jnp.transpose(received[1].reshape(recv_count, 3)).astype(jnp.float32)
    group_no = lax.axis_index("brick") * n_probe + lax.axis_index("probe")
    n_blocks, list_len = probe_list.shape
    probe_block = make_block(
        recv_rows,
        recv_pos,
        w_probe[:, 0, :],
        w_probe[:, 1, :],
        half_width,
        group_no,
        n_blocks,
        list_len,
        n_basis,
    )
    charges = lax.map(
        probe_block, (jnp.arange(n_blocks, dtype=jnp.int32), probe_list, probe_count)
    ).reshape(n_blocks * PB, half_width)
    mix_rows = lax.dynamic_slice_in_dim(w_mix, lax.axis_index("chan") * half_width, half_width, 0)
    mixed = lax.psum(jnp.dot(charges, mix_rows, preferred_element_type=jnp.float32), "chan")
    return jnp.sum(jax.nn.silu(mixed + b_mix) * w_out, axis=1)


def solution(mesh):
    in_specs = (
        P(("image", "brick", "probe"), "chan"),
        P(None, ("image", "brick", "probe")),
        P(None, ("image", "brick", "probe")),
        P(("image", "brick", "probe")),
        P(("image", "brick", "probe")),
        P(("image", "brick", "probe"), None),
        P(("image", "brick", "probe"), None),
        P(("image", "brick", "probe")),
        P(),
        P(),
        P(None, None, None, "chan"),
        P(None, None, None, "chan"),
        P(None, None, "chan"),
        P(),
        P(),
        P(),
    )
    out_specs = P(("image", "brick", "probe"))
    return jax.shard_map(
        per_device, mesh=mesh, in_specs=in_specs, out_specs=out_specs, check_vma=False
    )
```

profile of v0, /device:TPU:0, one launch (start us, length us, event | category | flops | bytes accessed | tf_op | source)
XLA Modules:
  0.0 28.2 jit_solution(10830102868108778274)
XLA Ops:
  0.0 2.3 %pack.1 = (bf16[8,104,128]{2,1,0:T(8,128)(2,1)}, bf16[448,128]{1,0:T(8,128)(2,1)}, f32[16,128]{1,0:T(8,128)}) custom-call(bf16[64,128]{1,0:T(8,128)(2,1)} %bitcast.15, f32[3,128]{1,0:T(4,128)} %atom_pos.1, f32[3,2048]{1,0:T(4,128)} %edge_vec.1, s32[16,128]{1,0:T(8,128)} %bitcast.16, s32[1,64]{1,0:T(1,128)} %bitcast.17, s32[1,32]{1,0:T(1,128)} %send.1, ...), custom_call_target="tpu_custom_call" | custom-call | tf_op jit(solution)/shard_map/pack/pallas_call | solution.py:163
  2.3 0.0 copy-start
  2.3 0.0 copy-start.2
  2.3 15.6 %all_to_all.5.data_mine = bf16[8,104,128]{2,1,0:T(8,128)(2,1)S(1)} all-to-all(bf16[8,104,128]{2,1,0:T(8,128)(2,1)} %get-tuple-element.11), channel_id=1, replica_groups=mesh['image'=2,'brick'=4,'probe'=2,'chan'=2] {'brick','probe'}, dimensions={0} | all-to-all | bytes 425984 | tf_op jit(solution)/shard_map/all_to_all | solution.py:536
  17.9 0.0 collective-permute-start
  17.9 0.0 copy-done
  17.9 0.5 %collective-permute-start.1 = (bf16[448,128]{1,0:T(8,128)(2,1)S(1)}, bf16[448,128]{1,0:T(8,128)(2,1)S(1)}, u32[]{:S(2)}, u32[]{:S(2)}) collective-permute-start(bf16[448,128]{1,0:T(8,128)(2,1)S(1)} %copy-done), channel_id=1, source_target_pairs={{0,1},{1,0},{2,3},{3,2},{4,5},{5,4},{6,7},{7,6},{8,9},{9,8},{10,11... | collective-permute-start | bytes 344072 | tf_op jit(solution)/shard_map/ppermute | solution.py:535
  18.4 0.0 copy-done.2
  18.4 0.0 copy-start.1
  18.4 0.0 copy-start.3
  18.4 1.4 %index.1 = (f32[16,512]{1,0:T(8,128)S(1)}, f32[128,128]{1,0:T(8,128)S(1)}, bf16[512,512]{1,0:T(8,128)(2,1)S(1)}) custom-call(bf16[8,104,128]{2,1,0:T(8,128)(2,1)S(1)} %all_to_all.5.data_mine, f32[16,128]{1,0:T(8,128)S(1)} %copy-done.2), custom_call_target="tpu_custom_call" | custom-call | tf_op jit(solution)/shard_map/index/pallas_call | solution.py:540
  19.9 0.0 collective-permute-done.1.weights_other
  19.9 0.0 collective-permute-done.data_other
  19.9 0.0 copy-done.1
  19.9 0.0 copy-done.3
  19.9 8.3 %density.1 = f32[1,512]{1,0:T(1,128)} custom-call(bf16[8,104,128]{2,1,0:T(8,128)(2,1)S(1)} %all_to_all.5.data_mine, bf16[8,104,128]{2,1,0:T(8,128)(2,1)S(1)} %collective-permute-done.data_other, bf16[448,128]{1,0:T(8,128)(2,1)S(1)} %copy-done, bf16[448,128]{1,0:T(8,128)(2,1)S(1)} %collective-permute-done.1.weights_other, f32[16,128]{1,0:T(8,128)S(1)} %copy-done.2, ...), custom_call_target="tpu_custom_call" | custom-call | tf_op jit(solution)/shard_map/density/pallas_call | solution.py:550
Async XLA Ops:
  2.3 15.6 %copy-start = (bf16[448,128]{1,0:T(8,128)(2,1)S(1)}, bf16[448,128]{1,0:T(8,128)(2,1)}, u32[]{:S(2)}) copy-start(bf16[448,128]{1,0:T(8,128)(2,1)} %get-tuple-element.12.weights_mine) | copy-start | bytes 344068
  2.3 16.1 %copy-start.2 = (f32[16,128]{1,0:T(8,128)S(1)}, f32[16,128]{1,0:T(8,128)}, u32[]{:S(2)}) copy-start(f32[16,128]{1,0:T(8,128)} %get-tuple-element.13.small) | copy-start | bytes 24580
  17.9 2.0 %collective-permute-start = (bf16[8,104,128]{2,1,0:T(8,128)(2,1)S(1)}, bf16[8,104,128]{2,1,0:T(8,128)(2,1)S(1)}, u32[]{:S(2)}, u32[]{:S(2)}) collective-permute-start(bf16[8,104,128]{2,1,0:T(8,128)(2,1)S(1)} %all_to_all.5.data_mine), channel_id=1, source_target_pairs={{0,1},{1,0},{2,3},{3,2},{4,5},{5,4},{6,7},{7,6},{8,9},{9,8},{10,11... | collective-permute-start | bytes 638984 | tf_op jit(solution)/shard_map/ppermute | solution.py:537
  17.9 2.0 %collective-permute-start.1 = (bf16[448,128]{1,0:T(8,128)(2,1)S(1)}, bf16[448,128]{1,0:T(8,128)(2,1)S(1)}, u32[]{:S(2)}, u32[]{:S(2)}) collective-permute-start(bf16[448,128]{1,0:T(8,128)(2,1)S(1)} %copy-done), channel_id=1, source_target_pairs={{0,1},{1,0},{2,3},{3,2},{4,5},{5,4},{6,7},{7,6},{8,9},{9,8},{10,11... | collective-permute-start | bytes 344072 | tf_op jit(solution)/shard_map/ppermute | solution.py:535
  18.4 1.5 %copy-start.1 = (bf16[2,128,128]{2,1,0:T(8,128)(2,1)S(1)}, bf16[2,128,128]{2,1,0:T(8,128)(2,1)}, u32[]{:S(2)}) copy-start(bf16[2,128,128]{2,1,0:T(8,128)(2,1)} %w_in.1) | copy-start | bytes 196612
  18.4 1.5 %copy-start.3 = (bf16[128,128]{1,0:T(8,128)(2,1)S(1)}, bf16[128,128]{1,0:T(8,128)(2,1)}, u32[]{:S(2)}) copy-start(bf16[128,128]{1,0:T(8,128)(2,1)} %w_mix.1) | copy-start | bytes 98308
where the time goes:
time: 28.5 us; the launch traced here: 28.2 us
  blocking collectives  15.6 us (55%)
  Pallas kernels  12 us (42%)
  starting transfers between devices  0.51 us (2%)
    all_to_all x1, blocking collectives, few_groups(): lax.all_to_all(data, ('brick', 'probe'), split_axis=0, concat_axis=0, til...  15.6 us
    pallas_call x1, Pallas kernels, few_groups(): pl.pallas_call(functools.partial(density_kernel, sizes), out_shape=jax.Sh...  8.3 us
    pallas_call x1, Pallas kernels, pack(): pl.pallas_call(functools.partial(pack_kernel, fan), out_shape=(jax.ShapeD...  2.29 us
    pallas_call x1, Pallas kernels, few_groups(): pl.pallas_call(functools.partial(index_kernel, sizes, w_in.shape[0] + 2),...  1.45 us
  transfers between devices with their start and end apart: 2, of which 0 were waited for; matrix products, arithmetic and copies ran while one was open for 0% of the time, Pallas kernels for 5%

commit v1 on v0

--- a/solution.py
+++ b/solution.py
@@ -73,8 +73,7 @@
 
 
 def pack_kernel(
-    fan, atom_s, atom_pos, edge_vec, edge_nbr, border, send, w_msg, w_rad, w_probe,
-    b_in, b_mix, w_out, probe_list, probe_count, data_out, weight_out, small_out, natural,
+    fan, atom_s, atom_pos, edge_vec, edge_nbr, border, send, data_out, natural
 ):
     half, atoms = atom_s.shape
     tiles = atoms * fan // LANES
@@ -143,6 +142,11 @@
         data_out[group, 0:half, :] = scalars
         data_out[group, half : half + 2 * fan, :] = edge_part
         data_out[group, half + 2 * fan :, :] = rest.astype(BF16)
+
+
+def weight_kernel(
+    w_msg, w_rad, w_probe, b_in, b_mix, w_out, probe_list, probe_count, weight_out, small_out
+):
     at = 0
     for piece in (b_in, b_mix, w_out, probe_list, probe_count):
         rows, cols = piece.shape
@@ -154,19 +158,12 @@
     weight_out[w_msg.shape[0] :, :] = radial
 
 
-def pack(
-    groups, atom_s, atom_pos, edge_vec, edge_nbr, border_index, send_index, w_msg, w_rad, w_probe,
-    b_in, b_mix, w_out, probe_list, probe_count,
-):
+def pack(copies, atom_s, atom_pos, edge_vec, edge_nbr, border_index, send_index):
     atoms, half = atom_s.shape
     fan = edge_nbr.shape[0] // atoms
     return pl.pallas_call(
         functools.partial(pack_kernel, fan),
-        out_shape=(
-            jax.ShapeDtypeStruct((groups, half + 4 * fan // 2 + 8, LANES), BF16),
-            jax.ShapeDtypeStruct((w_msg.size // LANES + half, LANES), BF16),
-            jax.ShapeDtypeStruct((SMALL, LANES), F32),
-        ),
+        out_shape=jax.ShapeDtypeStruct((copies, half + 4 * fan // 2 + 8, LANES), BF16),
         scratch_shapes=[pltpu.VMEM((LANES, LANES), F32)],
         name="pack",
     )(
@@ -176,6 +173,18 @@
         edge_nbr.reshape(-1, LANES),
         border_index.reshape(1, -1),
         send_index,
+    )
+
+
+def pack_weights(half, w_msg, w_rad, w_probe, b_in, b_mix, w_out, probe_list, probe_count):
+    return pl.pallas_call(
+        weight_kernel,
+        out_shape=(
+            jax.ShapeDtypeStruct((w_msg.size // LANES + half, LANES), BF16),
+            jax.ShapeDtypeStruct((SMALL, LANES), F32),
+        ),
+        name="pack_weights",
+    )(
         jnp.transpose(w_msg, (0, 2, 3, 1)).reshape(-1, LANES),
         jnp.transpose(w_rad, (0, 2, 1, 3)).reshape(-1, half),
         w_probe,
@@ -185,6 +194,10 @@
         probe_list,
         probe_count.reshape(1, -1),
     )
+
+
+def after_kernel(block, there, same_block):
+    pass
 
 
 def probe_grid(me, probes):
@@ -527,13 +540,23 @@
     cap = send_index.shape[1] // groups
     width = 2 * half
     every = groups * LANES
-    data, weights, small = pack(
-        groups, atom_s, atom_pos, edge_vec, edge_nbr, border_index, send_index, w_msg, w_rad, w_probe,
-        b_in, b_mix, w_out, probe_list, probe_count,
+    data = pack(groups, atom_s, atom_pos, edge_vec, edge_nbr, border_index, send_index)
+    weights, small = pack_weights(
+        half, w_msg, w_rad, w_probe, b_in, b_mix, w_out, probe_list, probe_count
     )
     swap = [(0, 1), (1, 0)]
     weights_other = lax.ppermute(weights, "chan", swap)
     mine = lax.all_to_all(data, ("brick", "probe"), split_axis=0, concat_axis=0, tiled=True)
+    anywhere = pl.BlockSpec(memory_space=pl.ANY)
+    mine = pl.pallas_call(
+        after_kernel,
+        out_shape=jax.ShapeDtypeStruct(mine.shape, BF16),
+        in_specs=[anywhere] * 2,
+        out_specs=anywhere,
+        input_output_aliases={0: 0},
+        compiler_params=pltpu.CompilerParams(vmem_limit_bytes=16 * 1024 * 1024),
+        name="after",
+    )(mine, weights_other)
     other = lax.ppermute(mine, "chan", swap)
     n_probes = probe_list.shape[0] * PB
     sizes = (groups, fan, rim, half, n_basis, cap, probe_list.shape[0])

time: 28.5 us -> 27.7 us (0.972)
  blocking collectives: 15.6 us -> 0 us
  starting transfers between devices: 0.51 us -> 7.26 us
  waiting for transfers between devices: 0.01 us -> 6.51 us
  Pallas kernels: 12 us -> 13.5 us
    all_to_all x1 -> x0, blocking collectives: 15.6 us -> none  [few_groups(): lax.all_to_all(data, ('brick', 'probe'), split_axis=0, concat_axis=0, til...]
    all_to_all x0 -> x1, starting transfers between devices: none -> 7.25 us  [few_groups(): lax.all_to_all(data, ('brick', 'probe'), split_axis=0, concat_axis=0, til...]
    all_to_all x0 -> x1, waiting for transfers between devices: none -> 4.98 us  [few_groups(): lax.all_to_all(data, ('brick', 'probe'), split_axis=0, concat_axis=0, til...]
    ppermute x1, waiting for transfers between devices: 0.01 us -> 1.53 us  [few_groups(): weights_other = lax.ppermute(weights, 'chan', swap)]
    pallas_call x1 -> x3, Pallas kernels: 2.29 us -> 3.74 us  [the longest x1 2.06 us: pack(): pl.pallas_call(functools.partial(pack_kernel, fan), out_shape=jax.ShapeDt...]
    ppermute x1, starting transfers between devices: 0.51 us -> 0.01 us  [few_groups(): weights_other = lax.ppermute(weights, 'chan', swap)]
  transfers between devices with their start and end apart: 2 -> 3, of which waited for: 0 -> 2; matrix products, arithmetic and copies ran while one was open for 0% -> 0% of each run, Pallas kernels for 5% -> 11%
where the time goes in v1:
time: 27.7 us; the launch traced here: 27.3 us
  Pallas kernels  13.5 us (49%)
  starting transfers between devices  7.26 us (26%)
  waiting for transfers between devices  6.51 us (24%)
    pallas_call x1, Pallas kernels, few_groups(): pl.pallas_call(functools.partial(density_kernel, sizes), out_shape=jax.Sh...  8.3 us
    all_to_all x1, starting transfers between devices, few_groups(): lax.all_to_all(data, ('brick', 'probe'), split_axis=0, concat_axis=0, til...  7.25 us
    all_to_all x1, waiting for transfers between devices, few_groups(): lax.all_to_all(data, ('brick', 'probe'), split_axis=0, concat_axis=0, til...  4.98 us
    pallas_call x1, Pallas kernels, pack(): pl.pallas_call(functools.partial(pack_kernel, fan), out_shape=jax.ShapeDt...  2.06 us
    pallas_call x1, Pallas kernels, pack_weights(): pl.pallas_call(weight_kernel, out_shape=(jax.ShapeDtypeStruct((w_msg.size...  1.68 us
    ppermute x1, waiting for transfers between devices, few_groups(): weights_other = lax.ppermute(weights, 'chan', swap)  1.53 us
    pallas_call x1, Pallas kernels, few_groups(): pl.pallas_call(functools.partial(index_kernel, sizes, w_in.shape[0] + 2),...  1.45 us
  transfers between devices with their start and end apart: 3, of which 2 were waited for; matrix products, arithmetic and copies ran while one was open for 0% of the time, Pallas kernels for 11%

profile of v1, /device:TPU:0, one launch (start us, length us, event | category | flops | bytes accessed | tf_op | source)
XLA Modules:
  0.0 27.3 jit_solution(3448510745783833340)
XLA Ops:
  0.0 2.1 %pack.1 = bf16[8,104,128]{2,1,0:T(8,128)(2,1)} custom-call(bf16[64,128]{1,0:T(8,128)(2,1)} %bitcast.15, f32[3,128]{1,0:T(4,128)} %atom_pos.1, f32[3,2048]{1,0:T(4,128)} %edge_vec.1, s32[16,128]{1,0:T(8,128)} %bitcast.16, s32[1,64]{1,0:T(1,128)} %bitcast.17, s32[1,32]{1,0:T(1,128)} %send.1), custom_call_target="tpu_custom_call" | custom-call | tf_op jit(solution)/shard_map/pack/pallas_call | solution.py:164
  2.1 7.3 %all-to-all-start = ((bf16[8,104,128]{2,1,0:T(8,128)(2,1)}), bf16[8,104,128]{2,1,0:T(8,128)(2,1)S(1)}, u32[]{:S(2)}, u32[]{:S(2)}) async-start(bf16[8,104,128]{2,1,0:T(8,128)(2,1)} %pack.1), calls=%async_computation | async-start | bytes 425984 | tf_op jit(solution)/shard_map/all_to_all | solution.py:549
  9.3 1.7 %pack_weights.1 = (bf16[448,128]{1,0:T(8,128)(2,1)}, f32[16,128]{1,0:T(8,128)}) custom-call(bf16[384,128]{1,0:T(8,128)(2,1)} %bitcast.13, bf16[96,64]{1,0:T(8,128)(2,1)} %bitcast.14, bf16[16,2,64]{2,1,0:T(2,128)(2,1)} %w_probe.1, f32[2,128]{1,0:T(2,128)} %b_in.1, f32[1,128]{1,0:T(1,128)} %bitcast.18, f32[1,128]{1,0:T(1,128)} %bitcast.19, ...), custom_call_target="tpu_custom_call" | custom-call | tf_op jit(solution)/shard_map/pack_weights/pallas_call | solution.py:180
  11.0 0.0 copy-start.2
  11.0 0.0 collective-permute-start
  11.0 1.5 %collective-permute-done.there.weights_other = bf16[448,128]{1,0:T(8,128)(2,1)S(1)} collective-permute-done((bf16[448,128]{1,0:T(8,128)(2,1)}, bf16[448,128]{1,0:T(8,128)(2,1)S(1)}, u32[]{:S(2)}, u32[]{:S(2)}) %collective-permute-start) | collective-permute-done | bytes 114720 | tf_op jit(solution)/shard_map/ppermute | solution.py:548
  12.5 5.0 %all-to-all-done.block = bf16[8,104,128]{2,1,0:T(8,128)(2,1)S(1)} async-done(((bf16[8,104,128]{2,1,0:T(8,128)(2,1)}), bf16[8,104,128]{2,1,0:T(8,128)(2,1)S(1)}, u32[]{:S(2)}, u32[]{:S(2)}) %all-to-all-start) | async-done | bytes 213024 | tf_op jit(solution)/shard_map/all_to_all | solution.py:549
  17.5 0.0 copy-start
  17.5 0.0 collective-permute-start.1
  17.5 0.0 copy-done.2
  17.5 0.0 copy-start.1
  17.5 0.0 copy-start.3
  17.5 1.4 %index.1 = (f32[16,512]{1,0:T(8,128)S(1)}, f32[128,128]{1,0:T(8,128)S(1)}, bf16[512,512]{1,0:T(8,128)(2,1)S(1)}) custom-call(bf16[8,104,128]{2,1,0:T(8,128)(2,1)S(1)} %after.1.data_mine, f32[16,128]{1,0:T(8,128)S(1)} %copy-done.2), custom_call_target="tpu_custom_call" | custom-call | tf_op jit(solution)/shard_map/index/pallas_call | solution.py:563
  19.0 0.0 collective-permute-done.1.data_other
  19.0 0.0 copy-done
  19.0 0.0 copy-done.1
  19.0 0.0 copy-done.3
  19.0 8.3 %density.1 = f32[1,512]{1,0:T(1,128)} custom-call(bf16[8,104,128]{2,1,0:T(8,128)(2,1)S(1)} %after.1.data_mine, bf16[8,104,128]{2,1,0:T(8,128)(2,1)S(1)} %collective-permute-done.1.data_other, bf16[448,128]{1,0:T(8,128)(2,1)S(1)} %copy-done, bf16[448,128]{1,0:T(8,128)(2,1)S(1)} %collective-permute-done.there.weights_other, f32[16,128]{1,0:T(8,128)S(1)} %copy-done.2, ...), custom_call_target="tpu_custom_call" | custom-call | tf_op jit(solution)/shard_map/density/pallas_call | solution.py:573
  (1 shorter events, 0.0 us)
Async XLA Ops:
  2.1 15.4 %all-to-all-start = ((bf16[8,104,128]{2,1,0:T(8,128)(2,1)}), bf16[8,104,128]{2,1,0:T(8,128)(2,1)S(1)}, u32[]{:S(2)}, u32[]{:S(2)}) async-start(bf16[8,104,128]{2,1,0:T(8,128)(2,1)} %pack.1), calls=%async_computation | async-start | bytes 425984 | tf_op jit(solution)/shard_map/all_to_all | solution.py:549
  11.0 6.5 %copy-start.2 = (f32[16,128]{1,0:T(8,128)S(1)}, f32[16,128]{1,0:T(8,128)}, u32[]{:S(2)}) copy-start(f32[16,128]{1,0:T(8,128)} %get-tuple-element.11.small) | copy-start | bytes 24580
  11.0 1.5 %collective-permute-start = (bf16[448,128]{1,0:T(8,128)(2,1)}, bf16[448,128]{1,0:T(8,128)(2,1)S(1)}, u32[]{:S(2)}, u32[]{:S(2)}) collective-permute-start(bf16[448,128]{1,0:T(8,128)(2,1)} %get-tuple-element.10.weights_mine), channel_id=1, source_target_pairs={{0,1},{1,0},{2,3},{3,2},{4,5},{5,4},{6,7},{7,6},{8,9},{9,8},{10,11... | collective-permute-start | bytes 344072 | tf_op jit(solution)/shard_map/ppermute | solution.py:548
  17.5 1.5 %copy-start = (bf16[448,128]{1,0:T(8,128)(2,1)S(1)}, bf16[448,128]{1,0:T(8,128)(2,1)}, u32[]{:S(2)}) copy-start(bf16[448,128]{1,0:T(8,128)(2,1)} %get-tuple-element.10.weights_mine) | copy-start | bytes 344068
  17.5 1.5 %collective-permute-start.1 = (bf16[8,104,128]{2,1,0:T(8,128)(2,1)S(1)}, bf16[8,104,128]{2,1,0:T(8,128)(2,1)S(1)}, u32[]{:S(2)}, u32[]{:S(2)}) collective-permute-start(bf16[8,104,128]{2,1,0:T(8,128)(2,1)S(1)} %after.1.data_mine), channel_id=1, source_target_pairs={{0,1},{1,0},{2,3},{3,2},{4,5},{5,4},{6,7},{7,6},{8,9},{9,8},{10,11... | collective-permute-start | bytes 638984 | tf_op jit(solution)/shard_map/ppermute | solution.py:560
  17.5 1.5 %copy-start.1 = (bf16[2,128,128]{2,1,0:T(8,128)(2,1)S(1)}, bf16[2,128,128]{2,1,0:T(8,128)(2,1)}, u32[]{:S(2)}) copy-start(bf16[2,128,128]{2,1,0:T(8,128)(2,1)} %w_in.1) | copy-start | bytes 196612
  17.5 1.5 %copy-start.3 = (bf16[128,128]{1,0:T(8,128)(2,1)S(1)}, bf16[128,128]{1,0:T(8,128)(2,1)}, u32[]{:S(2)}) copy-start(bf16[128,128]{1,0:T(8,128)(2,1)} %w_mix.1) | copy-start | bytes 98308

commit v2 on v1

--- a/solution.py
+++ b/solution.py
@@ -368,6 +368,9 @@
     radial_at = weights.shape[1] - half
     radial_all = jnp.concatenate([weights[c, radial_at:, :] for c in range(2)], axis=0)
 
+    some = LANES // 2
+    crowded = jnp.max(facts[8:9, 0:groups]) > some
+
     received = groups * cap
     edges = received * fan
     per_group = fan * cap
@@ -420,7 +423,6 @@
     radial_rows = jnp.concatenate([jnp.zeros((2 * width, LANES + 2 * rim), BF16), radial_ac], axis=1)
     blank = jnp.zeros((2 * width, n_basis), BF16)
 
-    some = LANES // 2
     step = fan // 2
 
     def update(group, first_slot):
@@ -471,7 +473,7 @@
                 acc = acc + block[:width]
                 for x in range(3):
                     acc_vec[x] = acc_vec[x] + block[width:] * vec[x][k : k + 1]
-        acc, *acc_vec = [(a[:, :some] + a[:, some:]) / root_fan for a in [acc] + acc_vec]
+        acc, *acc_vec = [(a[:, :some] + a[:, some:]) * (1.0 / root_fan) for a in [acc] + acc_vec]
         return jnp.concatenate([own_scalars + acc] + acc_vec, axis=0)
 
     for group in range(groups):
@@ -479,7 +481,7 @@
         state = jnp.concatenate([state, jnp.zeros_like(state)], axis=1)
         state1[:, group * LANES : (group + 1) * LANES] = state.astype(BF16)
 
-    @pl.when(jnp.max(facts[8:9, 0:groups]) > some)
+    @pl.when(crowded)
     def _():
         for group in range(groups):
 

time: 27.7 us -> 27.6 us (level)
  no operation moved by 1% of the time
where the time goes in v2:
time: 27.6 us; the launch traced here: 27.3 us
  Pallas kernels  13.5 us (49%)
  starting transfers between devices  7.26 us (26%)
  waiting for transfers between devices  6.51 us (24%)
    pallas_call x1, Pallas kernels, few_groups(): pl.pallas_call(functools.partial(density_kernel, sizes), out_shape=jax.Sh...  8.27 us
    all_to_all x1, starting transfers between devices, few_groups(): lax.all_to_all(data, ('brick', 'probe'), split_axis=0, concat_axis=0, til...  7.25 us
    all_to_all x1, waiting for transfers between devices, few_groups(): lax.all_to_all(data, ('brick', 'probe'), split_axis=0, concat_axis=0, til...  4.98 us
    pallas_call x1, Pallas kernels, pack(): pl.pallas_call(functools.partial(pack_kernel, fan), out_shape=jax.ShapeDt...  2.06 us
    pallas_call x1, Pallas kernels, pack_weights(): pl.pallas_call(weight_kernel, out_shape=(jax.ShapeDtypeStruct((w_msg.size...  1.68 us
    ppermute x1, waiting for transfers between devices, few_groups(): weights_other = lax.ppermute(weights, 'chan', swap)  1.53 us
    pallas_call x1, Pallas kernels, few_groups(): pl.pallas_call(functools.partial(index_kernel, sizes, w_in.shape[0] + 2),...  1.45 us
  transfers between devices with their start and end apart: 3, of which 2 were waited for; matrix products, arithmetic and copies ran while one was open for 0% of the time, Pallas kernels for 11%

profile of v2, /device:TPU:0, one launch (start us, length us, event | category | flops | bytes accessed | tf_op | source)
XLA Modules:
  0.0 27.3 jit_solution(9751471938543802032)
XLA Ops:
  0.0 2.1 %pack.1 = bf16[8,104,128]{2,1,0:T(8,128)(2,1)} custom-call(bf16[64,128]{1,0:T(8,128)(2,1)} %bitcast.15, f32[3,128]{1,0:T(4,128)} %atom_pos.1, f32[3,2048]{1,0:T(4,128)} %edge_vec.1, s32[16,128]{1,0:T(8,128)} %bitcast.16, s32[1,64]{1,0:T(1,128)} %bitcast.17, s32[1,32]{1,0:T(1,128)} %send.1), custom_call_target="tpu_custom_call" | custom-call | tf_op jit(solution)/shard_map/pack/pallas_call | solution.py:164
  2.1 7.3 %all-to-all-start = ((bf16[8,104,128]{2,1,0:T(8,128)(2,1)}), bf16[8,104,128]{2,1,0:T(8,128)(2,1)S(1)}, u32[]{:S(2)}, u32[]{:S(2)}) async-start(bf16[8,104,128]{2,1,0:T(8,128)(2,1)} %pack.1), calls=%async_computation | async-start | bytes 425984 | tf_op jit(solution)/shard_map/all_to_all | solution.py:551
  9.3 1.7 %pack_weights.1 = (bf16[448,128]{1,0:T(8,128)(2,1)}, f32[16,128]{1,0:T(8,128)}) custom-call(bf16[384,128]{1,0:T(8,128)(2,1)} %bitcast.13, bf16[96,64]{1,0:T(8,128)(2,1)} %bitcast.14, bf16[16,2,64]{2,1,0:T(2,128)(2,1)} %w_probe.1, f32[2,128]{1,0:T(2,128)} %b_in.1, f32[1,128]{1,0:T(1,128)} %bitcast.18, f32[1,128]{1,0:T(1,128)} %bitcast.19, ...), custom_call_target="tpu_custom_call" | custom-call | tf_op jit(solution)/shard_map/pack_weights/pallas_call | solution.py:180
  11.0 0.0 copy-start.2
  11.0 0.0 collective-permute-start
  11.0 1.5 %collective-permute-done.there.weights_other = bf16[448,128]{1,0:T(8,128)(2,1)S(1)} collective-permute-done((bf16[448,128]{1,0:T(8,128)(2,1)}, bf16[448,128]{1,0:T(8,128)(2,1)S(1)}, u32[]{:S(2)}, u32[]{:S(2)}) %collective-permute-start) | collective-permute-done | bytes 114720 | tf_op jit(solution)/shard_map/ppermute | solution.py:550
  12.5 5.0 %all-to-all-done.block = bf16[8,104,128]{2,1,0:T(8,128)(2,1)S(1)} async-done(((bf16[8,104,128]{2,1,0:T(8,128)(2,1)}), bf16[8,104,128]{2,1,0:T(8,128)(2,1)S(1)}, u32[]{:S(2)}, u32[]{:S(2)}) %all-to-all-start) | async-done | bytes 213024 | tf_op jit(solution)/shard_map/all_to_all | solution.py:551
  17.5 0.0 copy-start
  17.5 0.0 collective-permute-start.1
  17.5 0.0 copy-done.2
  17.5 0.0 copy-start.1
  17.5 0.0 copy-start.3
  17.5 1.4 %index.1 = (f32[16,512]{1,0:T(8,128)S(1)}, f32[128,128]{1,0:T(8,128)S(1)}, bf16[512,512]{1,0:T(8,128)(2,1)S(1)}) custom-call(bf16[8,104,128]{2,1,0:T(8,128)(2,1)S(1)} %after.1.data_mine, f32[16,128]{1,0:T(8,128)S(1)} %copy-done.2), custom_call_target="tpu_custom_call" | custom-call | tf_op jit(solution)/shard_map/index/pallas_call | solution.py:565
  19.0 0.0 collective-permute-done.1.data_other
  19.0 0.0 copy-done
  19.0 0.0 copy-done.1
  19.0 0.0 copy-done.3
  19.0 8.3 %density.1 = f32[1,512]{1,0:T(1,128)} custom-call(bf16[8,104,128]{2,1,0:T(8,128)(2,1)S(1)} %after.1.data_mine, bf16[8,104,128]{2,1,0:T(8,128)(2,1)S(1)} %collective-permute-done.1.data_other, bf16[448,128]{1,0:T(8,128)(2,1)S(1)} %copy-done, bf16[448,128]{1,0:T(8,128)(2,1)S(1)} %collective-permute-done.there.weights_other, f32[16,128]{1,0:T(8,128)S(1)} %copy-done.2, ...), custom_call_target="tpu_custom_call" | custom-call | tf_op jit(solution)/shard_map/density/pallas_call | solution.py:575
  (1 shorter events, 0.0 us)
Async XLA Ops:
  2.1 15.4 %all-to-all-start = ((bf16[8,104,128]{2,1,0:T(8,128)(2,1)}), bf16[8,104,128]{2,1,0:T(8,128)(2,1)S(1)}, u32[]{:S(2)}, u32[]{:S(2)}) async-start(bf16[8,104,128]{2,1,0:T(8,128)(2,1)} %pack.1), calls=%async_computation | async-start | bytes 425984 | tf_op jit(solution)/shard_map/all_to_all | solution.py:551
  11.0 6.5 %copy-start.2 = (f32[16,128]{1,0:T(8,128)S(1)}, f32[16,128]{1,0:T(8,128)}, u32[]{:S(2)}) copy-start(f32[16,128]{1,0:T(8,128)} %get-tuple-element.11.small) | copy-start | bytes 24580
  11.0 1.5 %collective-permute-start = (bf16[448,128]{1,0:T(8,128)(2,1)}, bf16[448,128]{1,0:T(8,128)(2,1)S(1)}, u32[]{:S(2)}, u32[]{:S(2)}) collective-permute-start(bf16[448,128]{1,0:T(8,128)(2,1)} %get-tuple-element.10.weights_mine), channel_id=1, source_target_pairs={{0,1},{1,0},{2,3},{3,2},{4,5},{5,4},{6,7},{7,6},{8,9},{9,8},{10,11... | collective-permute-start | bytes 344072 | tf_op jit(solution)/shard_map/ppermute | solution.py:550
  17.5 1.5 %copy-start = (bf16[448,128]{1,0:T(8,128)(2,1)S(1)}, bf16[448,128]{1,0:T(8,128)(2,1)}, u32[]{:S(2)}) copy-start(bf16[448,128]{1,0:T(8,128)(2,1)} %get-tuple-element.10.weights_mine) | copy-start | bytes 344068
  17.5 1.5 %collective-permute-start.1 = (bf16[8,104,128]{2,1,0:T(8,128)(2,1)S(1)}, bf16[8,104,128]{2,1,0:T(8,128)(2,1)S(1)}, u32[]{:S(2)}, u32[]{:S(2)}) collective-permute-start(bf16[8,104,128]{2,1,0:T(8,128)(2,1)S(1)} %after.1.data_mine), channel_id=1, source_target_pairs={{0,1},{1,0},{2,3},{3,2},{4,5},{5,4},{6,7},{7,6},{8,9},{9,8},{10,11... | collective-permute-start | bytes 638984 | tf_op jit(solution)/shard_map/ppermute | solution.py:562
  17.5 1.5 %copy-start.1 = (bf16[2,128,128]{2,1,0:T(8,128)(2,1)S(1)}, bf16[2,128,128]{2,1,0:T(8,128)(2,1)}, u32[]{:S(2)}) copy-start(bf16[2,128,128]{2,1,0:T(8,128)(2,1)} %w_in.1) | copy-start | bytes 196612
  17.5 1.5 %copy-start.3 = (bf16[128,128]{1,0:T(8,128)(2,1)S(1)}, bf16[128,128]{1,0:T(8,128)(2,1)}, u32[]{:S(2)}) copy-start(bf16[128,128]{1,0:T(8,128)(2,1)} %w_mix.1) | copy-start | bytes 98308

commit v3 on v1

--- a/solution.py
+++ b/solution.py
@@ -13,7 +13,7 @@
 LANES = 128
 FEW_GROUPS = 8
 SMALL = 16
-TOGETHER = 2
+TOGETHER = 4
 ROOT = (2.0 * math.log2(math.e)) ** 0.5
 F32 = jnp.float32
 BF16 = jnp.bfloat16

time: 27.7 us -> 27.7 us (level)
  no operation moved by 1% of the time
where the time goes in v3:
time: 27.7 us; the launch traced here: 27.3 us
  Pallas kernels  13.5 us (49%)
  starting transfers between devices  7.26 us (26%)
  waiting for transfers between devices  6.51 us (24%)
    pallas_call x1, Pallas kernels, few_groups(): pl.pallas_call(functools.partial(density_kernel, sizes), out_shape=jax.Sh...  8.3 us
    all_to_all x1, starting transfers between devices, few_groups(): lax.all_to_all(data, ('brick', 'probe'), split_axis=0, concat_axis=0, til...  7.25 us
    all_to_all x1, waiting for transfers between devices, few_groups(): lax.all_to_all(data, ('brick', 'probe'), split_axis=0, concat_axis=0, til...  4.98 us
    pallas_call x1, Pallas kernels, pack(): pl.pallas_call(functools.partial(pack_kernel, fan), out_shape=jax.ShapeDt...  2.06 us
    pallas_call x1, Pallas kernels, pack_weights(): pl.pallas_call(weight_kernel, out_shape=(jax.ShapeDtypeStruct((w_msg.size...  1.68 us
    ppermute x1, waiting for transfers between devices, few_groups(): weights_other = lax.ppermute(weights, 'chan', swap)  1.53 us
    pallas_call x1, Pallas kernels, few_groups(): pl.pallas_call(functools.partial(index_kernel, sizes, w_in.shape[0] + 2),...  1.45 us
  transfers between devices with their start and end apart: 3, of which 2 were waited for; matrix products, arithmetic and copies ran while one was open for 0% of the time, Pallas kernels for 11%

profile of v3, /device:TPU:0, one launch (start us, length us, event | category | flops | bytes accessed | tf_op | source)
XLA Modules:
  0.0 27.3 jit_solution(12482569983183689214)
XLA Ops:
  0.0 2.1 %pack.1 = bf16[8,104,128]{2,1,0:T(8,128)(2,1)} custom-call(bf16[64,128]{1,0:T(8,128)(2,1)} %bitcast.15, f32[3,128]{1,0:T(4,128)} %atom_pos.1, f32[3,2048]{1,0:T(4,128)} %edge_vec.1, s32[16,128]{1,0:T(8,128)} %bitcast.16, s32[1,64]{1,0:T(1,128)} %bitcast.17, s32[1,32]{1,0:T(1,128)} %send.1), custom_call_target="tpu_custom_call" | custom-call | tf_op jit(solution)/shard_map/pack/pallas_call | solution.py:164
  2.1 7.3 %all-to-all-start = ((bf16[8,104,128]{2,1,0:T(8,128)(2,1)}), bf16[8,104,128]{2,1,0:T(8,128)(2,1)S(1)}, u32[]{:S(2)}, u32[]{:S(2)}) async-start(bf16[8,104,128]{2,1,0:T(8,128)(2,1)} %pack.1), calls=%async_computation | async-start | bytes 425984 | tf_op jit(solution)/shard_map/all_to_all | solution.py:549
  9.3 1.7 %pack_weights.1 = (bf16[448,128]{1,0:T(8,128)(2,1)}, f32[16,128]{1,0:T(8,128)}) custom-call(bf16[384,128]{1,0:T(8,128)(2,1)} %bitcast.13, bf16[96,64]{1,0:T(8,128)(2,1)} %bitcast.14, bf16[16,2,64]{2,1,0:T(2,128)(2,1)} %w_probe.1, f32[2,128]{1,0:T(2,128)} %b_in.1, f32[1,128]{1,0:T(1,128)} %bitcast.18, f32[1,128]{1,0:T(1,128)} %bitcast.19, ...), custom_call_target="tpu_custom_call" | custom-call | tf_op jit(solution)/shard_map/pack_weights/pallas_call | solution.py:180
  11.0 0.0 copy-start.2
  11.0 0.0 collective-permute-start
  11.0 1.5 %collective-permute-done.there.weights_other = bf16[448,128]{1,0:T(8,128)(2,1)S(1)} collective-permute-done((bf16[448,128]{1,0:T(8,128)(2,1)}, bf16[448,128]{1,0:T(8,128)(2,1)S(1)}, u32[]{:S(2)}, u32[]{:S(2)}) %collective-permute-start) | collective-permute-done | bytes 114720 | tf_op jit(solution)/shard_map/ppermute | solution.py:548
  12.5 5.0 %all-to-all-done.block = bf16[8,104,128]{2,1,0:T(8,128)(2,1)S(1)} async-done(((bf16[8,104,128]{2,1,0:T(8,128)(2,1)}), bf16[8,104,128]{2,1,0:T(8,128)(2,1)S(1)}, u32[]{:S(2)}, u32[]{:S(2)}) %all-to-all-start) | async-done | bytes 213024 | tf_op jit(solution)/shard_map/all_to_all | solution.py:549
  17.5 0.0 copy-start
  17.5 0.0 collective-permute-start.1
  17.5 0.0 copy-done.2
  17.5 0.0 copy-start.1
  17.5 0.0 copy-start.3
  17.5 1.4 %index.1 = (f32[16,512]{1,0:T(8,128)S(1)}, f32[128,128]{1,0:T(8,128)S(1)}, bf16[512,512]{1,0:T(8,128)(2,1)S(1)}) custom-call(bf16[8,104,128]{2,1,0:T(8,128)(2,1)S(1)} %after.1.data_mine, f32[16,128]{1,0:T(8,128)S(1)} %copy-done.2), custom_call_target="tpu_custom_call" | custom-call | tf_op jit(solution)/shard_map/index/pallas_call | solution.py:563
  19.0 0.0 collective-permute-done.1.data_other
  19.0 0.0 copy-done
  19.0 0.0 copy-done.1
  19.0 0.0 copy-done.3
  19.0 8.3 %density.1 = f32[1,512]{1,0:T(1,128)} custom-call(bf16[8,104,128]{2,1,0:T(8,128)(2,1)S(1)} %after.1.data_mine, bf16[8,104,128]{2,1,0:T(8,128)(2,1)S(1)} %collective-permute-done.1.data_other, bf16[448,128]{1,0:T(8,128)(2,1)S(1)} %copy-done, bf16[448,128]{1,0:T(8,128)(2,1)S(1)} %collective-permute-done.there.weights_other, f32[16,128]{1,0:T(8,128)S(1)} %copy-done.2, ...), custom_call_target="tpu_custom_call" | custom-call | tf_op jit(solution)/shard_map/density/pallas_call | solution.py:573
  (1 shorter events, 0.0 us)
Async XLA Ops:
  2.1 15.4 %all-to-all-start = ((bf16[8,104,128]{2,1,0:T(8,128)(2,1)}), bf16[8,104,128]{2,1,0:T(8,128)(2,1)S(1)}, u32[]{:S(2)}, u32[]{:S(2)}) async-start(bf16[8,104,128]{2,1,0:T(8,128)(2,1)} %pack.1), calls=%async_computation | async-start | bytes 425984 | tf_op jit(solution)/shard_map/all_to_all | solution.py:549
  11.0 6.5 %copy-start.2 = (f32[16,128]{1,0:T(8,128)S(1)}, f32[16,128]{1,0:T(8,128)}, u32[]{:S(2)}) copy-start(f32[16,128]{1,0:T(8,128)} %get-tuple-element.11.small) | copy-start | bytes 24580
  11.0 1.5 %collective-permute-start = (bf16[448,128]{1,0:T(8,128)(2,1)}, bf16[448,128]{1,0:T(8,128)(2,1)S(1)}, u32[]{:S(2)}, u32[]{:S(2)}) collective-permute-start(bf16[448,128]{1,0:T(8,128)(2,1)} %get-tuple-element.10.weights_mine), channel_id=1, source_target_pairs={{0,1},{1,0},{2,3},{3,2},{4,5},{5,4},{6,7},{7,6},{8,9},{9,8},{10,11... | collective-permute-start | bytes 344072 | tf_op jit(solution)/shard_map/ppermute | solution.py:548
  17.5 1.5 %copy-start = (bf16[448,128]{1,0:T(8,128)(2,1)S(1)}, bf16[448,128]{1,0:T(8,128)(2,1)}, u32[]{:S(2)}) copy-start(bf16[448,128]{1,0:T(8,128)(2,1)} %get-tuple-element.10.weights_mine) | copy-start | bytes 344068
  17.5 1.5 %collective-permute-start.1 = (bf16[8,104,128]{2,1,0:T(8,128)(2,1)S(1)}, bf16[8,104,128]{2,1,0:T(8,128)(2,1)S(1)}, u32[]{:S(2)}, u32[]{:S(2)}) collective-permute-start(bf16[8,104,128]{2,1,0:T(8,128)(2,1)S(1)} %after.1.data_mine), channel_id=1, source_target_pairs={{0,1},{1,0},{2,3},{3,2},{4,5},{5,4},{6,7},{7,6},{8,9},{9,8},{10,11... | collective-permute-start | bytes 638984 | tf_op jit(solution)/shard_map/ppermute | solution.py:560
  17.5 1.5 %copy-start.1 = (bf16[2,128,128]{2,1,0:T(8,128)(2,1)S(1)}, bf16[2,128,128]{2,1,0:T(8,128)(2,1)}, u32[]{:S(2)}) copy-start(bf16[2,128,128]{2,1,0:T(8,128)(2,1)} %w_in.1) | copy-start | bytes 196612
  17.5 1.5 %copy-start.3 = (bf16[128,128]{1,0:T(8,128)(2,1)S(1)}, bf16[128,128]{1,0:T(8,128)(2,1)}, u32[]{:S(2)}) copy-start(bf16[128,128]{1,0:T(8,128)(2,1)} %w_mix.1) | copy-start | bytes 98308
